TPU v7x, 32 devices: a whole 2x2x4 slice. The times are simulated.
32 devices in a mesh: row: 4 (over z), col: 8 (over y, x, core).
Axes of the slice: x: 2, y: 2, z: 4, core: 2. Of those that a mesh axis runs over, the one named last changes fastest.
Arguments:
- embeds: bfloat16 [6144, 768], P('col'), may hold values from -6 to 6
- labels: bfloat16 [6144, 1000], P('col'), may hold values from -6 to 6
- sharpness: float32 [6144], P('col'), may hold values from 0.5 to 100
- pattern: int32 [48, 16], P('col'), may hold values from 0 to 47, as said below
- mask_pos: int32 [6144, 50], P('col'), may hold values from 0 to 2047, as said below
Outputs:
- propagated: bfloat16 [6144, 1000], P('col', 'row')
Inputs may be any that keep to these rules, and one draw needn't show every extreme that they name: `pattern`: split the row blocks into runs of 6 and the slots into runs of 4; within one run of row blocks and one run of slots, ids that lie in the same run of 6 block ids are equal. `mask_pos`: the 50 positions of a row are distinct; position k * 128 + m names row m of the row block's k-th candidate block.
All inputs are finite; a program needn't handle non-finite values.
Results may differ from a plain program's by a relative error of at most 0.012.
Values may be sent and summed in bfloat16 or wider, within the bound.
A program may use at most 128 MiB of HBM per device.

v0:
```python
import math

import jax
import jax.numpy as jnp
from jax import lax
from jax.sharding import PartitionSpec as P

BLOCK = 128
SLOTS = 16


mixing = 0.75
lowest_logit = -1e30


def body(embeds, labels, sharpness, pattern, mask_pos):
    rows_here, width = embeds.shape
    classes = labels.shape[1]
    n_col = lax.axis_size("col")
    n_row = lax.axis_size("row")
    row_pos = lax.axis_index("row")
    blocks_here = rows_here // BLOCK
    slots_here = SLOTS // n_row
    span = slots_here * BLOCK
    my_slots = lax.dynamic_slice_in_dim(pattern, row_pos * slots_here, slots_here, 1)
    owners = my_slots // blocks_here
    local_ids = my_slots % blocks_here
    peers = jnp.arange(n_col, dtype=jnp.int32)
    wanted = jnp.max(jnp.where(owners[..., None] == peers, local_ids[..., None], 0), axis=(0, 1))
    requested = lax.all_to_all(wanted, "col", split_axis=0, concat_axis=0, tiled=True)
    embedding_tiles = embeds.reshape(blocks_here, BLOCK, width)
    lab_blocks = labels.reshape(blocks_here, BLOCK, classes)
    send_emb = embedding_tiles[requested]
    send_lab = lab_blocks[requested]
    shifted = mask_pos - row_pos * span
    shifted = jnp.where((shifted >= 0) & (shifted < span), shifted, span)
    row_ids = jnp.arange(rows_here, dtype=jnp.int32)[:, None]
    in_mask = (
        jnp.zeros((rows_here, span), jnp.float32).at[row_ids, shifted].set(1.0, mode="drop") > 0.5
    )
    in_mask = in_mask.reshape(blocks_here, BLOCK, span)

    def propagate_using(weight_matrix, fetched_lab):
        candidate_ids = fetched_lab[owners].reshape(blocks_here, span, classes)
        blended_rows = jnp.einsum(
            "tmg,tgh->tmh", weight_matrix, candidate_ids, preferred_element_type=jnp.float32
        )
        return blended_rows.reshape(rows_here, classes)

    fetched_emb, fetched_lab = (
        lax.all_to_all(send_emb, "col", split_axis=0, concat_axis=0, tiled=True),
        lax.all_to_all(send_lab, "col", split_axis=0, concat_axis=0, tiled=True),
    )
    candidate_ids = fetched_emb[owners].reshape(blocks_here, span, width)
    scores = jnp.einsum(
        "evg,erg->evr", embedding_tiles, candidate_ids, preferred_element_type=jnp.float32
    ) / math.sqrt(width)
    logits = scores * sharpness.reshape(blocks_here, BLOCK, 1)
    local_max = jnp.max(jnp.where(in_mask, logits, lowest_logit), axis=2)
    top = lax.pmax(local_max, "row")
    totals = lax.psum(
        jnp.sum(jnp.where(in_mask, jnp.exp(logits - top[..., None]), 0.0), axis=2), "row"
    )
    weight_matrix = jnp.where(
        in_mask, jnp.exp(logits - top[..., None]) / totals[..., None], 0.0
    ).astype(jnp.bfloat16)
    partial_one = propagate_using(weight_matrix, fetched_lab)
    summed = lax.psum(partial_one.astype(jnp.bfloat16), "row").astype(jnp.float32)
    spread = (mixing * summed + (1.0 - mixing) * labels.astype(jnp.float32)).astype(jnp.bfloat16)
    send_spread = spread.reshape(blocks_here, BLOCK, classes)[requested]
    fetched_spread = lax.all_to_all(send_spread, "col", split_axis=0, concat_axis=0, tiled=True)
    partial_two = propagate_using(weight_matrix, fetched_spread)
    share = lax.psum_scatter(
        partial_two.astype(jnp.bfloat16), "row", scatter_dimension=1, tiled=True
    ).astype(jnp.float32)
    per_device = classes // n_row
    seed_part = lax.dynamic_slice_in_dim(labels, row_pos * per_device, per_device, 1)
    return (mixing * share + (1.0 - mixing) * seed_part.astype(jnp.float32)).astype(jnp.bfloat16)


def solution(mesh):
    placed = (P("col", None), P("col", None), P("col"), P("col", None), P("col", None))
    return jax.shard_map(
        body, mesh=mesh, in_specs=placed, out_specs=P("col", "row"), check_vma=False
    )
```

profile of v0, /device:TPU:1, one launch (start us, length us, event | category | flops | bytes accessed | tf_op | source)
XLA Modules:
  0.0 442.9 jit_solution(11335543893860007553)
XLA Ops:
  7.6 9.0 %all_to_all.27 = s32[8,1,1]{2,1,0:T(1,128)S(1)} all-to-all(s32[8,1,1]{2,1,0:T(1,128)S(1)} %copy.62), channel_id=1, replica_groups=mesh['row'=4,'col'=8] {'col'}, dimensions={0} | all-to-all | bytes 64 | tf_op jit(solution)/shard_map/all_to_all | solution.py:30
  18.6 4.2 all-to-all-start.1
  22.8 2.6 copy.66
  25.5 2.6 copy.67
  29.0 141.9 %scatter_custom_fusion = f32[393216]{0:T(1024)} fusion(s32[38400]{0:T(1024)S(1)} %reshape.127, f32[38400]{0:T(1024)S(1)} %broadcast.66, f32[]{:T(128)} %constant.20.clone.1), kind=kCustom, calls=%fused_computation.18 | custom fusion | bytes 1572868
  170.8 3.5 gather_fusion.2
  175.6 4.2 all-to-all-start.2
  186.7 4.5 %gather_fusion.1 = bf16[24,128,768]{2,1,0:T(8,128)(2,1)} fusion(bf16[8,128,768]{2,1,0:T(8,128)(2,1)} %copy-done.1, s32[1024]{0:T(1024)S(1)} %pad_clamp_fusion), kind=kCustom, calls=%fused_computation.1 | custom fusion | bytes 9437280 | tf_op jit(solution)/shard_map/gather | solution.py:54
  191.2 4.9 %fusion = (f32[6,128]{1,0:T(8,128)S(1)}, f32[6,512,128]{2,1,0:T(8,128)}) fusion(pred[6,128,512]{1,2,0:T(32,128)(4,1)} %copy.65, f32[6,128]{1,0:T(8,128)S(1)} %multiply_bitcast_fusion, bf16[6,512,768]{2,1,0:T(8,128)(2,1)} %bitcast.45, bf16[6,128,768]{2,1,0:T(8,128)(2,1)S(1)} %bitcast.38), kind=kOutput, calls=%fused_computation.12 | convolution fusion | flops 605158656 | bytes 7870464 | tf_op jit(solution)/shard_map/evg,erg->evr/dot_general | solution.py:55
  196.2 9.9 %pmax.7 = f32[6,128]{1,0:T(8,128)S(1)} all-reduce(f32[6,128]{1,0:T(8,128)S(1)} %get-tuple-element.8), channel_id=1, replica_groups=mesh['row'=4,'col'=8] {'row'}, use_global_device_ids=true, to_apply=%region_3.4 | all-reduce | flops 768 | bytes 6144 | tf_op jit(solution)/shard_map/pmax | solution.py:60
  208.0 6.6 %psum.14 = f32[6,128]{1,0:T(8,128)S(1)} all-reduce(f32[6,128]{1,0:T(8,128)S(1)} %select_reduce_fusion), channel_id=1, replica_groups=mesh['row'=4,'col'=8] {'row'}, use_global_device_ids=true, to_apply=%region_5.6 | all-reduce | flops 768 | bytes 6144 | tf_op jit(solution)/shard_map/psum | solution.py:61
  214.6 4.4 gather_fusion.3
  219.0 8.8 %copy.68 = bf16[24,128,1000]{2,1,0:T(8,128)(2,1)} copy(bf16[24,128,1000]{1,2,0:T(8,128)(2,1)} %gather_fusion.3) | data formatting | bytes 12288000 | tf_op jit(solution)/shard_map/gather | solution.py:44
  227.8 6.2 %convolution_convert_fusion.1 = bf16[6,128,1000]{1,2,0:T(8,128)(2,1)} fusion(bf16[6,512,1000]{2,1,0:T(8,128)(2,1)} %bitcast.41, pred[6,128,512]{1,2,0:T(32,128)(4,1)S(1)} %copy-done.5, f32[6,512,128]{2,1,0:T(8,128)S(1)} %copy-done.3, f32[6,128]{1,0:T(8,128)S(1)} %psum.14, f32[6,128]{1,0:T(8,128)S(1)} %pmax.7), kind=kOutput, calls=%fused_computation.9 | convolution fusion | flops 788772864 | bytes 9652224 | tf_op jit(solution)/shard_map/tmg,tgh->tmh/dot_general | solution.py:45
  234.0 2.7 copy.71
  236.9 71.1 %all-reduce.4.cloned.1.call-done = bf16[768,1000]{1,0:T(8,128)(2,1)} async-done(((bf16[768,1000]{1,0:T(8,128)(2,1)}), bf16[768,1000]{1,0:T(8,128)(2,1)}) %all-reduce.4.cloned.1.call-update) | async-done | bytes 1536016 | tf_op jit(solution)/shard_map/psum | solution.py:68
  308.1 3.3 add_convert_fusion
  315.4 30.5 %all_to_all.28 = bf16[8,128,1000]{1,2,0:T(8,128)(2,1)S(1)} all-to-all(bf16[8,128,1000]{1,2,0:T(8,128)(2,1)} %gather_fusion.4), channel_id=1, replica_groups=mesh['row'=4,'col'=8] {'col'}, dimensions={0} | all-to-all | bytes 4096000 | tf_op jit(solution)/shard_map/all_to_all | solution.py:71
  345.9 4.4 gather_fusion.5
  350.3 8.8 %copy.74 = bf16[24,128,1000]{2,1,0:T(8,128)(2,1)} copy(bf16[24,128,1000]{1,2,0:T(8,128)(2,1)} %gather_fusion.5) | data formatting | bytes 12288000 | tf_op jit(solution)/shard_map/gather | solution.py:44
  359.0 6.2 %convolution_convert_fusion = bf16[6,128,1000]{1,2,0:T(8,128)(2,1)} fusion(bf16[6,512,1000]{2,1,0:T(8,128)(2,1)} %bitcast.40, pred[6,128,512]{1,2,0:T(32,128)(4,1)S(1)} %copy-done.6, f32[6,512,128]{2,1,0:T(8,128)S(1)} %copy-done.4, f32[6,128]{1,0:T(8,128)S(1)} %psum.14, f32[6,128]{1,0:T(8,128)S(1)} %pmax.7), kind=kOutput, calls=%fused_computation.8 | convolution fusion | flops 788772864 | bytes 9652224 | tf_op jit(solution)/shard_map/tmg,tgh->tmh/dot_general | solution.py:45
  365.3 2.6 copy.77
  369.7 63.9 %all-reduce.6.cloned.1.call-done = bf16[768,1000]{1,0:T(8,128)(2,1)} async-done(((bf16[768,1000]{1,0:T(8,128)(2,1)}), bf16[768,1000]{1,0:T(8,128)(2,1)}) %all-reduce.6.cloned.1.call-update) | async-done | bytes 1536016
  433.7 2.4 add_convert_fusion.1
  (55 shorter events, 19.5 us)
Async XLA Ops:
  6.5 10.3 %copy-start = (bf16[768,768]{1,0:T(8,128)(2,1)S(1)}, bf16[768,768]{1,0:T(8,128)(2,1)}, u32[]{:S(2)}) copy-start(bf16[768,768]{1,0:T(8,128)(2,1)} %param.5) | copy-start | bytes 3538948
  18.6 155.8 %all-to-all-start.1 = ((bf16[8,128,768]{2,1,0:T(8,128)(2,1)}), bf16[8,128,768]{2,1,0:T(8,128)(2,1)S(1)}, u32[]{:S(2)}, u32[]{:S(2)}) async-start(bf16[8,128,768]{2,1,0:T(8,128)(2,1)} %gather_fusion), calls=%async_computation.1 | async-start | bytes 3145728 | tf_op jit(solution)/shard_map/all_to_all | solution.py:51
  25.4 2.6 copy-start.7
  25.4 2.7 copy-start.10
  25.5 2.8 copy-start.9
  174.4 1.2 copy-start.1
  175.6 39.1 %all-to-all-start.2 = ((bf16[8,128,1000]{1,2,0:T(8,128)(2,1)}), bf16[8,128,1000]{1,2,0:T(8,128)(2,1)S(1)}, u32[]{:S(2)}, u32[]{:S(2)}) async-start(bf16[8,128,1000]{1,2,0:T(8,128)(2,1)} %gather_fusion.2), calls=%async_computation.2 | async-start | bytes 4096000 | tf_op jit(solution)/shard_map/all_to_all | solution.py:52
  179.8 6.9 %copy-start.8 = (f32[768]{0:T(1024)S(1)}, f32[768]{0:T(1024)}, u32[]{:S(2)}) copy-start(f32[768]{0:T(1024)} %param.7) | copy-start | bytes 9220
  179.8 128.3 %all-reduce.4.cloned.1.call-start = ((), (), s32[]{:S(2)}) async-start(), calls=%async_computation.4 | async-start | bytes 3145728 | tf_op jit(solution)/shard_map/psum | solution.py:68
  219.0 8.8 %copy-start.3 = (f32[6,512,128]{2,1,0:T(8,128)S(1)}, f32[6,512,128]{2,1,0:T(8,128)}, u32[]{:S(2)}) copy-start(f32[6,512,128]{2,1,0:T(8,128)} %get-tuple-element.9) | copy-start | bytes 4718596
  219.0 8.8 %copy-start.5 = (pred[6,128,512]{1,2,0:T(32,128)(4,1)S(1)}, pred[6,128,512]{1,2,0:T(32,128)(4,1)}, u32[]{:S(2)}) copy-start(pred[6,128,512]{1,2,0:T(32,128)(4,1)} %copy.65) | copy-start | bytes 1179652
  234.0 74.1 %copy-start.2 = (bf16[768,1000]{1,0:T(8,128)(2,1)S(1)}, bf16[768,1000]{1,0:T(8,128)(2,1)}, u32[]{:S(2)}) copy-start(bf16[768,1000]{1,0:T(8,128)(2,1)} %copy.66) | copy-start | bytes 4608004
  236.7 197.0 %all-reduce.6.cloned.1.call-start = ((), (), s32[]{:S(2)}) async-start(), calls=%async_computation.5 | async-start | bytes 3145728
  350.3 8.8 %copy-start.4 = (f32[6,512,128]{2,1,0:T(8,128)S(1)}, f32[6,512,128]{2,1,0:T(8,128)}, u32[]{:S(2)}) copy-start(f32[6,512,128]{2,1,0:T(8,128)} %get-tuple-element.9) | copy-start | bytes 4718596
  350.3 8.8 %copy-start.6 = (pred[6,128,512]{1,2,0:T(32,128)(4,1)S(1)}, pred[6,128,512]{1,2,0:T(32,128)(4,1)}, u32[]{:S(2)}) copy-start(pred[6,128,512]{1,2,0:T(32,128)(4,1)} %copy.65) | copy-start | bytes 1179652
  367.8 0.7 copy-start.11
Sparse Core Ops, SparseCore 0:
  236.8 71.1 all-reduce.3
  368.0 65.6 all-reduce.5
where the time goes:
time: 446 us; the launch traced here: 443 us
  local copies, waits for them, and re-layouts  200 us (45%)
  waiting for transfers between devices  135 us (30%)
  blocking collectives  56 us (13%)
  matrix products  17.4 us (4%)
  between operations  14.2 us (3%)
  other arithmetic  11.5 us (3%)
  starting transfers between devices  8.64 us (2%)
    unnamed x30, local copies, waits for them, and re-layouts  147 us
    psum x1, waiting for transfers between devices, body(): lax.psum(partial_one.astype(jnp.bfloat16), 'row').astype(jnp.float32)  71.1 us
    unnamed x3, waiting for transfers between devices  64 us
    all_to_all x1, blocking collectives, body(): lax.all_to_all(send_spread, 'col', split_axis=0, concat_axis=0, tiled=True)  30.5 us
    gather x4, local copies, waits for them, and re-layouts, propagate_using(): candidate_ids = fetched_lab[owners].reshape(blocks_here, span, classes)  26.3 us
    dot_general x2, matrix products, propagate_using(): jnp.einsum('tmg,tgh->tmh', weight_matrix, candidate_ids, preferred_elemen...  12.4 us
    pmax x1, blocking collectives, body(): top = lax.pmax(local_max, 'row')  9.91 us
    all_to_all x1, blocking collectives, body(): lax.all_to_all(wanted, 'col', split_axis=0, concat_axis=0, tiled=True)  8.98 us
  transfers between devices with their start and end apart: 4, of which 2 were waited for; matrix products, arithmetic and copies ran while one was open for 38% of the time, Pallas kernels for 0%

commit v1 on v0

v1 whole, which is shorter than its diff:
```python
import functools
import math

import jax
import jax.numpy as jnp
from jax import lax
from jax.experimental import pallas as pl
from jax.experimental.pallas import tpu as pltpu
from jax.sharding import PartitionSpec as P

BLOCK = 128
SLOTS = 16
LANES = 128
HALF = 64
MESH = pl.DeviceIdType.MESH

mixing = 0.75
lowest_logit = -1e30


def lane_pick(values, index):
    return jnp.take_along_axis(values, index, axis=1, mode="promise_in_bounds")


def kernel(
    n_row, n_col, neighbours, width,
    pattern_ref, query_ref, emb_ref, lab_ref, pos_ref, sharp_ref, out_ref,
    emb_all, lab_all, spread_all, code, part, rs_buf, w_all, dense,
    local_sem, emb_send, emb_recv, lab_send, lab_recv, spread_send, spread_recv,
    rs_send, rs_recv, w_send, w_recv,
):
    me_row = lax.axis_index("row")
    me_col = lax.axis_index("col")
    blocks = lab_ref.shape[0]
    pairs = blocks // 2
    packed = pos_ref.shape[0]
    chunk = packed // n_row
    classes = lab_ref.shape[2]

    def row_peer(d):
        return lax.rem(me_row + d, n_row)

    def col_peer(d):
        return lax.rem(me_col + d, n_col)

    barrier = pltpu.get_barrier_semaphore()
    for d in range(1, n_col):
        pl.semaphore_signal(barrier, inc=1, device_id=(me_row, col_peer(d)), device_id_type=MESH)
    for d in range(1, n_row):
        pl.semaphore_signal(barrier, inc=1, device_id=(row_peer(d), me_col), device_id_type=MESH)
    pl.semaphore_wait(barrier, n_col + n_row - 2)

    mine = pl.ds(me_col * blocks, blocks)

    def gather_copies(src, whole, send, recv):
        return [
            pltpu.make_async_remote_copy(
                src_ref=src,
                dst_ref=whole.at[mine],
                send_sem=send.at[d],
                recv_sem=recv.at[d],
                device_id=(me_row, col_peer(d)),
                device_id_type=MESH,
            )
            for d in range(1, n_col)
        ]

    emb_copies = gather_copies(emb_ref, emb_all, emb_send, emb_recv)
    lab_copies = gather_copies(lab_ref, lab_all, lab_send, lab_recv)
    for copy in emb_copies:
        copy.start()
    own_emb = pltpu.make_async_copy(emb_ref, emb_all.at[mine], local_sem.at[0])
    own_emb.start()
    for copy in lab_copies:
        copy.start()
    own_lab = pltpu.make_async_copy(lab_ref, lab_all.at[mine], local_sem.at[1])
    own_lab.start()

    lane8 = lax.broadcasted_iota(jnp.int32, (8, LANES), 1)

    def encode(g, _):
        rows = pl.ds(pl.multiple_of(g * 8, 8), 8)
        pos = pos_ref[rows, :]
        inside = pos & (BLOCK - 1)
        slot = pos >> 7
        number = (lane8 & (HALF - 1)) << ((slot & 3) * 8)
        words = [jnp.where((slot >> 2) == q, number, 0) for q in range(4)]
        for h in range(2):
            acc = [jnp.full((8, LANES), 0x40404040 * h, jnp.int32) for _ in range(4)]
            for n in range(1, neighbours + 1):
                at = h * HALF + n
                hit = jnp.broadcast_to(inside[:, at : at + 1], (8, LANES)) == lane8
                for q in range(4):
                    word = jnp.broadcast_to(words[q][:, at : at + 1], (8, LANES))
                    acc[q] = acc[q] | jnp.where(hit, word, 0)
            for q in range(4):
                code[h * 4 + q, rows, :] = acc[q]
        return 0

    lax.fori_loop(0, packed // 8, encode, 0)

    own_emb.wait()
    for copy in emb_copies:
        copy.wait()

    lower = lax.broadcasted_iota(jnp.int32, (BLOCK, LANES), 1) < HALF

    def score(b, _):
        rows = pl.ds(pl.multiple_of(b * BLOCK, BLOCK), BLOCK)
        pos = pos_ref[rows, :]
        inside = pos & (BLOCK - 1)
        slot = pos >> 7
        acc = jnp.zeros((BLOCK, LANES), jnp.float32)
        for k in range(0, SLOTS, 2):
            picked = [None, None]
            for h in range(2):
                block = b + h * pairs
                q_rows = pl.ds(pl.multiple_of(block * BLOCK, BLOCK), BLOCK)
                cand = jnp.concatenate(
                    [emb_all[pattern_ref[block, k]], emb_all[pattern_ref[block, k + 1]]], axis=1
                )
                picked[h] = jnp.dot(query_ref[q_rows, :], cand, preferred_element_type=jnp.float32)
            for u in range(2):
                cols = slice(u * LANES, (u + 1) * LANES)
                got = jnp.where(
                    lower, lane_pick(picked[0][:, cols], inside), lane_pick(picked[1][:, cols], inside)
                )
                acc = jnp.where(slot == k + u, got, acc)
        part[rows, :] = acc
        return 0

    lax.fori_loop(0, pairs, score, 0)

    rs_copies = [
        pltpu.make_async_remote_copy(
            src_ref=part.at[pl.ds(row_peer(d) * chunk, chunk)],
            dst_ref=rs_buf.at[d],
            send_sem=rs_send.at[d],
            recv_sem=rs_recv.at[d],
            device_id=(row_peer(d), me_col),
            device_id_type=MESH,
        )
        for d in range(1, n_row)
    ]
    for copy in rs_copies:
        copy.start()
    my_rows = pl.ds(pl.multiple_of(me_row * chunk, chunk), chunk)
    total = part[my_rows, :]
    for d, copy in enumerate(rs_copies):
        copy.wait()
        total = total + rs_buf[d + 1]

    low = lax.broadcasted_iota(jnp.int32, (chunk, LANES), 1) < HALF
    valid = pos_ref[my_rows, :] >= 0
    logits = jnp.where(valid, total / math.sqrt(width) * sharp_ref[my_rows, :], lowest_logit)

    def by_half(reduce, values, neutral):
        first = reduce(jnp.where(low, values, neutral), axis=1, keepdims=True)
        second = reduce(jnp.where(low, neutral, values), axis=1, keepdims=True)
        return jnp.where(low, first, second)

    top = by_half(jnp.max, logits, lowest_logit)
    expo = jnp.where(valid, jnp.exp(logits - top), 0.0)
    sums = by_half(jnp.sum, expo, 0.0)
    w_all[my_rows, :] = (expo / sums).astype(jnp.bfloat16)

    w_copies = [
        pltpu.make_async_remote_copy(
            src_ref=w_all.at[my_rows],
            dst_ref=w_all.at[my_rows],
            send_sem=w_send.at[d],
            recv_sem=w_recv.at[d],
            device_id=(row_peer(d), me_col),
            device_id_type=MESH,
        )
        for d in range(1, n_row)
    ]
    for copy in w_copies:
        copy.start()
    for copy in w_copies:
        copy.wait()
    own_lab.wait()
    for copy in lab_copies:
        copy.wait()

    def blend(acc, block):
        return (mixing * acc + (1.0 - mixing) * lab_ref[block].astype(jnp.float32)).astype(
            jnp.bfloat16
        )

    def first_round(b, _):
        rows = pl.ds(pl.multiple_of(b * BLOCK, BLOCK), BLOCK)
        weights = w_all[rows, :].astype(jnp.float32)
        for h in range(2):
            block = b + h * pairs
            acc = jnp.zeros((BLOCK, classes), jnp.float32)
            for k in range(0, SLOTS, 2):
                pieces = []
                for u in range(k, k + 2):
                    index = (code[h * 4 + u // 4, rows, :] >> (8 * (u % 4))) & 0x7F
                    pieces.append(lane_pick(weights, index).astype(jnp.bfloat16))
                wide = jnp.concatenate(pieces, axis=1)
                dense[block, :, k * BLOCK : (k + 2) * BLOCK] = wide
                cand = jnp.concatenate(
                    [lab_all[pattern_ref[block, k]], lab_all[pattern_ref[block, k + 1]]], axis=0
                )
                acc += jnp.dot(wide, cand, preferred_element_type=jnp.float32)
            spread_all[me_col * blocks + block] = blend(acc, block)
        return 0

    lax.fori_loop(0, pairs, first_round, 0)

    spread_copies = gather_copies(spread_all.at[mine], spread_all, spread_send, spread_recv)
    for copy in spread_copies:
        copy.start()
    for copy in spread_copies:
        copy.wait()

    def second_round(block, _):
        acc = jnp.zeros((BLOCK, classes), jnp.float32)
        for k in range(0, SLOTS, 2):
            cand = jnp.concatenate(
                [spread_all[pattern_ref[block, k]], spread_all[pattern_ref[block, k + 1]]], axis=0
            )
            acc += jnp.dot(
                dense[block, :, k * BLOCK : (k + 2) * BLOCK], cand, preferred_element_type=jnp.float32
            )
        out_ref[block] = blend(acc, block)
        return 0

    lax.fori_loop(0, blocks, second_round, 0)


def body(embeds, labels, sharpness, pattern, mask_pos):
    rows_here, width = embeds.shape
    classes = labels.shape[1]
    neighbours = mask_pos.shape[1]
    n_col = lax.axis_size("col")
    n_row = lax.axis_size("row")
    row_pos = lax.axis_index("row")
    blocks = rows_here // BLOCK
    packed = rows_here // 2
    features = width // n_row
    per_device = classes // n_row
    wide = -(-per_device // LANES) * LANES

    query = lax.dynamic_slice_in_dim(embeds, row_pos * features, features, 1)
    emb = query.reshape(blocks, BLOCK, features).transpose(0, 2, 1)
    lab = lax.dynamic_slice_in_dim(labels, row_pos * per_device, per_device, 1)
    lab = jnp.pad(lab, ((0, 0), (0, wide - per_device))).reshape(blocks, BLOCK, wide)
    pos = jnp.pad(mask_pos, ((0, 0), (1, HALF - 1 - neighbours)), constant_values=-1)
    pos = jnp.concatenate([pos[:packed], pos[packed:]], axis=1)
    sharp = jnp.concatenate(
        [
            jnp.broadcast_to(sharpness[:packed, None], (packed, HALF)),
            jnp.broadcast_to(sharpness[packed:, None], (packed, HALF)),
        ],
        axis=1,
    )
    total_blocks = n_col * blocks
    vmem = pl.BlockSpec(memory_space=pltpu.VMEM)
    out = pl.pallas_call(
        functools.partial(kernel, n_row, n_col, neighbours, width),
        out_shape=jax.ShapeDtypeStruct((blocks, BLOCK, wide), jnp.bfloat16),
        in_specs=[pl.BlockSpec(memory_space=pltpu.SMEM)] + [vmem] * 5,
        out_specs=vmem,
        scratch_shapes=[
            pltpu.VMEM((total_blocks, features, BLOCK), jnp.bfloat16),
            pltpu.VMEM((total_blocks, BLOCK, wide), jnp.bfloat16),
            pltpu.VMEM((total_blocks, BLOCK, wide), jnp.bfloat16),
            pltpu.VMEM((8, packed, LANES), jnp.int32),
            pltpu.VMEM((packed, LANES), jnp.float32),
            pltpu.VMEM((n_row, packed // n_row, LANES), jnp.float32),
            pltpu.VMEM((packed, LANES), jnp.bfloat16),
            pltpu.VMEM((blocks, BLOCK, SLOTS * BLOCK), jnp.bfloat16),
            pltpu.SemaphoreType.DMA((2,)),
        ]
        + [pltpu.SemaphoreType.DMA((n_col,))] * 6
        + [pltpu.SemaphoreType.DMA((n_row,))] * 4,
        compiler_params=pltpu.CompilerParams(
            collective_id=0, has_side_effects=True, vmem_limit_bytes=48 * 1024 * 1024
        ),
    )(pattern, query, emb, lab, pos, sharp)
    return out.reshape(rows_here, wide)[:, :per_device]


def solution(mesh):
    placed = (P("col", None), P("col", None), P("col"), P("col", None), P("col", None))
    return jax.shard_map(
        body, mesh=mesh, in_specs=placed, out_specs=P("col", "row"), check_vma=False
    )
```

time: 446 us -> 112 us (0.25)
  local copies, waits for them, and re-layouts: 200 us -> 3.58 us
  waiting for transfers between devices: 135 us -> 0 us
  Pallas kernels: 0 us -> 108 us
  blocking collectives: 56 us -> 0 us
  matrix products: 17.4 us -> 0 us
  between operations: 14.2 us -> 0.13 us
  other arithmetic: 11.5 us -> 0.25 us
  starting transfers between devices: 8.64 us -> 0 us
    unnamed x30 -> x11, local copies, waits for them, and re-layouts: 147 us -> 1.47 us
    pallas_call x0 -> x1, Pallas kernels: none -> 108 us  [body(): pl.pallas_call(functools.partial(kernel, n_row, n_col, neighbours, width)...]
    psum x1 -> x0, waiting for transfers between devices: 71.1 us -> none  [body(): lax.psum(partial_one.astype(jnp.bfloat16), 'row').astype(jnp.float32)]
    unnamed x3 -> x0, waiting for transfers between devices: 64 us -> none
    all_to_all x2 -> x0, blocking collectives: 39.4 us -> none  [the longest x1 30.5 us: body(): lax.all_to_all(send_spread, 'col', split_axis=0, concat_axis=0, tiled=True)]
    gather x8 -> x0, local copies, waits for them, and re-layouts: 38.3 us -> none  [the longest x4 26.3 us: propagate_using(): candidate_ids = fetched_lab[owners].reshape(blocks_here, span, classes)]
    dot_general x3 -> x0, matrix products: 17.4 us -> none  [the longest x2 12.4 us: propagate_using(): jnp.einsum('tmg,tgh->tmh', weight_matrix, candidate_ids, preferred_elemen...]
    pmax x1 -> x0, blocking collectives: 9.91 us -> none  [body(): top = lax.pmax(local_max, 'row')]
  transfers between devices with their start and end apart: 4 -> 0, of which waited for: 2 -> 0; matrix products, arithmetic and copies ran while one was open for 38% -> 0% of each run, Pallas kernels for 0% -> 0%
where the time goes in v1:
time: 112 us
  Pallas kernels  108 us (96%)
  local copies, waits for them, and re-layouts  3.58 us (3%)
    pallas_call x1, Pallas kernels, body(): pl.pallas_call(functools.partial(kernel, n_row, n_col, neighbours, width)...  108 us

profile of v1, /device:TPU:1, one launch (start us, length us, event | category | flops | bytes accessed | tf_op | source)
XLA Modules:
  0.0 112.2 jit_solution(16062089950741044234)
XLA Ops:
  0.0 0.0 copy-start
  0.0 1.4 %constant_dynamic-slice_fusion.1.query_ref = bf16[768,192]{1,0:T(8,128)(2,1)S(1)} fusion(bf16[768,768]{1,0:T(8,128)(2,1)} %param.5, s32[]{:T(128)S(6)} %select_n.6), kind=kLoop, calls=%fused_computation.5 | loop fusion | bytes 589828 | tf_op jit(solution)/shard_map/dynamic_slice | solution.py:247
  1.4 0.0 copy-start.2
  1.4 0.2 copy.9
  1.6 0.0 copy-done
  1.6 0.1 constant_dynamic-slice_fusion
  1.7 0.2 copy.14
  1.9 0.0 copy-start.3
  1.9 0.1 pad.8.clone
  2.0 0.0 copy-start.1
  2.0 0.4 copy-done.2
  2.3 0.2 copy.11
  2.5 0.2 pad_slice_fusion.1
  2.7 0.1 pad_add_fusion.pos_ref
  2.8 0.0 copy-done.3
  2.8 0.1 broadcast_in_dim.4
  2.9 0.1 broadcast_in_dim.5
  3.1 0.1 pad_maximum_fusion.sharp_ref
  3.2 0.0 copy-done.1
  3.2 108.2 %shard_map.55 = bf16[6,128,256]{2,1,0:T(8,128)(2,1)S(1)} custom-call(s32[6,16]{1,0:T(8,128)S(1)} %copy-done.1, bf16[768,192]{1,0:T(8,128)(2,1)S(1)} %constant_dynamic-slice_fusion.1.query_ref, bf16[6,192,128]{2,1,0:T(8,128)(2,1)S(1)} %bitcast.8, bf16[6,128,256]{2,1,0:T(8,128)(2,1)S(1)} %bitcast.6, s32[384,128]{1,0:T(8,128)S(1)} %pad_add_fusion.pos_ref, ...), custom_call_target="tpu_custom_call" | custom-call | tf_op jit(solution)/shard_map/pallas_call | solution.py:262
  111.4 0.7 copy.16
  (1 shorter events, 0.0 us)
Async XLA Ops:
  0.0 1.6 %copy-start = (bf16[768,1000]{0,1:T(8,128)(2,1)S(1)}, bf16[768,1000]{0,1:T(8,128)(2,1)}, u32[]{:S(2)}) copy-start(bf16[768,1000]{0,1:T(8,128)(2,1)} %param.6) | copy-start | bytes 4608004
  1.4 1.0 copy-start.2
  1.9 0.9 copy-start.3
  2.0 1.2 %copy-start.1 = (s32[6,16]{1,0:T(8,128)S(1)}, s32[6,16]{1,0:T(8,128)}, u32[]{:S(2)}) copy-start(s32[6,16]{1,0:T(8,128)} %pattern_ref.1) | copy-start | bytes 1156

commit v2 on v1

--- a/solution.py
+++ b/solution.py
@@ -22,10 +22,118 @@
     return jnp.take_along_axis(values, index, axis=1, mode="promise_in_bounds")
 
 
+class DirectGather:
+    def __init__(self, own, whole, send, recv, local, n_col):
+        row, me = lax.axis_index("row"), lax.axis_index("col")
+        blocks = whole.shape[0] // n_col
+        mine = pl.ds(me * blocks, blocks)
+        self.local = None if own is None else pltpu.make_async_copy(own, whole.at[mine], local)
+        self.copies = [
+            pltpu.make_async_remote_copy(
+                src_ref=whole.at[mine] if own is None else own,
+                dst_ref=whole.at[mine],
+                send_sem=send.at[d],
+                recv_sem=recv.at[d],
+                device_id=(row, lax.rem(me + d, n_col)),
+                device_id_type=MESH,
+            )
+            for d in range(1, n_col)
+        ]
+
+    def start(self):
+        for copy in self.copies:
+            copy.start()
+        if self.local is not None:
+            self.local.start()
+
+    def start_half(self, half):
+        if half == 1:
+            self.start()
+
+    def forward_first(self):
+        pass
+
+    def forward_rest(self):
+        pass
+
+    def finish(self):
+        if self.local is not None:
+            self.local.wait()
+        for copy in self.copies:
+            copy.wait()
+
+
+class PairwiseGather:
+    def __init__(self, own, whole, send, recv, local, n_col):
+        row, me = lax.axis_index("row"), lax.axis_index("col")
+        blocks = whole.shape[0] // n_col
+        part = blocks // 2
+        core, x, y = me % 2, (me // 2) % 2, me // 4
+        sib = me + 1 - 2 * core
+        xn = me + 2 - 4 * x
+        yn = me + 4 - 8 * y
+        diagonal = xn + yn - me
+        plan = [
+            (me, 0, xn), (me, 1, yn), (me, 1, xn), (me, 0, yn), (me, 0, sib), (me, 1, sib),
+            (xn, 0, yn), (yn, 1, xn), (xn, 0, sib), (yn, 1, sib), (xn, 1, sib), (yn, 0, sib),
+            (diagonal, 0, sib), (diagonal, 1, sib),
+        ]
+        self.local = None
+        if own is not None:
+            self.local = pltpu.make_async_copy(own, whole.at[pl.ds(me * blocks, blocks)], local)
+        self.copies = []
+        for i, (owner, half, target) in enumerate(plan):
+            there = whole.at[pl.ds(owner * blocks + half * part, part)]
+            src = there if own is None or i >= 6 else own.at[pl.ds(half * part, part)]
+            self.copies.append(
+                pltpu.make_async_remote_copy(
+                    src_ref=src,
+                    dst_ref=there,
+                    send_sem=send.at[i],
+                    recv_sem=recv.at[i],
+                    device_id=(row, target),
+                    device_id_type=MESH,
+                )
+            )
+
+    def start(self):
+        for i in range(6):
+            self.copies[i].start()
+        if self.local is not None:
+            self.local.start()
+
+    def start_half(self, half):
+        for i in ((0, 3, 4), (1, 2, 5))[half]:
+            self.copies[i].start()
+
+    def pass_on(self, arrived, onward):
+        self.copies[arrived].wait_recv()
+        for i in onward:
+            self.copies[i].start()
+
+    def forward_first(self):
+        self.pass_on(0, (6, 8))
+        self.pass_on(1, (7, 9))
+
+    def forward_rest(self):
+        self.pass_on(2, (10,))
+        self.pass_on(3, (11,))
+        self.pass_on(6, (12,))
+        self.pass_on(7, (13,))
+
+    def finish(self):
+        if self.local is not None:
+            self.local.wait()
+        for i in (4, 5, 8, 9, 10, 11, 12, 13):
+            self.copies[i].wait_recv()
+        for copy in self.copies:
+            copy.wait_send()
+
+
 def kernel(
     n_row, n_col, neighbours, width,
-    pattern_ref, query_ref, emb_ref, lab_ref, pos_ref, sharp_ref, out_ref,
-    emb_all, lab_all, spread_all, code, part, rs_buf, w_all, dense,
+    pattern_ref, query_ref, emb_ref, lab_ref, pos_ref, post_ref, sharp_ref, out_ref,
+    emb_all, lab_all, spread_all, code, turned, number, part, rs_buf, w_all, dense,
     local_sem, emb_send, emb_recv, lab_send, lab_recv, spread_send, spread_recv,
     rs_send, rs_recv, w_send, w_recv,
 ):
@@ -50,58 +158,44 @@
         pl.semaphore_signal(barrier, inc=1, device_id=(row_peer(d), me_col), device_id_type=MESH)
     pl.semaphore_wait(barrier, n_col + n_row - 2)
 
-    mine = pl.ds(me_col * blocks, blocks)
-
-    def gather_copies(src, whole, send, recv):
-        return [
-            pltpu.make_async_remote_copy(
-                src_ref=src,
-                dst_ref=whole.at[mine],
-                send_sem=send.at[d],
-                recv_sem=recv.at[d],
-                device_id=(me_row, col_peer(d)),
-                device_id_type=MESH,
-            )
-            for d in range(1, n_col)
-        ]
-
-    emb_copies = gather_copies(emb_ref, emb_all, emb_send, emb_recv)
-    lab_copies = gather_copies(lab_ref, lab_all, lab_send, lab_recv)
-    for copy in emb_copies:
-        copy.start()
-    own_emb = pltpu.make_async_copy(emb_ref, emb_all.at[mine], local_sem.at[0])
-    own_emb.start()
-    for copy in lab_copies:
-        copy.start()
-    own_lab = pltpu.make_async_copy(lab_ref, lab_all.at[mine], local_sem.at[1])
-    own_lab.start()
-
-    lane8 = lax.broadcasted_iota(jnp.int32, (8, LANES), 1)
-
-    def encode(g, _):
-        rows = pl.ds(pl.multiple_of(g * 8, 8), 8)
-        pos = pos_ref[rows, :]
-        inside = pos & (BLOCK - 1)
+    gather = PairwiseGather if n_col == 8 else DirectGather
+    emb_gather = gather(emb_ref, emb_all, emb_send, emb_recv, local_sem.at[0], n_col)
+    lab_gather = gather(lab_ref, lab_all, lab_send, lab_recv, local_sem.at[1], n_col)
+    spread_gather = gather(None, spread_all, spread_send, spread_recv, None, n_col)
+
+    tile = 32
+    emb_gather.start()
+
+    def encode(block, _):
+        cols = pl.ds(pl.multiple_of(block * BLOCK, BLOCK), BLOCK)
+        pos = post_ref[:, cols]
         slot = pos >> 7
-        number = (lane8 & (HALF - 1)) << ((slot & 3) * 8)
-        words = [jnp.where((slot >> 2) == q, number, 0) for q in range(4)]
-        for h in range(2):
-            acc = [jnp.full((8, LANES), 0x40404040 * h, jnp.int32) for _ in range(4)]
+        value = lax.broadcasted_iota(jnp.int32, (HALF, BLOCK), 0) << ((slot & 3) * 8)
+        number[4] = pos & (BLOCK - 1)
+        for q in range(4):
+            number[q] = jnp.where((slot >> 2) == q, value, 0)
+        side = block // pairs
+        for at in range(0, BLOCK, tile):
+            here = at + lax.broadcasted_iota(jnp.int32, (tile, BLOCK), 0)
+            acc = [jnp.full((tile, BLOCK), 0x40404040 * side, jnp.int32) for _ in range(4)]
             for n in range(1, neighbours + 1):
-                at = h * HALF + n
-                hit = jnp.broadcast_to(inside[:, at : at + 1], (8, LANES)) == lane8
+                hit = jnp.broadcast_to(number[4, n : n + 1, :], (tile, BLOCK)) == here
                 for q in range(4):
-                    word = jnp.broadcast_to(words[q][:, at : at + 1], (8, LANES))
+                    word = jnp.broadcast_to(number[q, n : n + 1, :], (tile, BLOCK))
                     acc[q] = acc[q] | jnp.where(hit, word, 0)
             for q in range(4):
-                code[h * 4 + q, rows, :] = acc[q]
+                turned[q, at : at + tile, :] = acc[q]
+        rows = pl.ds(pl.multiple_of((block - side * pairs) * BLOCK, BLOCK), BLOCK)
+        for q in range(4):
+            code[side * 4 + q, rows, :] = turned[q].T
         return 0
 
-    lax.fori_loop(0, packed // 8, encode, 0)
-
-    own_emb.wait()
-    for copy in emb_copies:
-        copy.wait()
+    lax.fori_loop(0, pairs, encode, 0)
+    emb_gather.forward_first()
+    lax.fori_loop(pairs, blocks, encode, 0)
+    emb_gather.forward_rest()
+    lab_gather.start()
+    emb_gather.finish()
 
     lower = lax.broadcasted_iota(jnp.int32, (BLOCK, LANES), 1) < HALF
 
@@ -144,6 +238,7 @@
     ]
     for copy in rs_copies:
         copy.start()
+    lab_gather.forward_first()
     my_rows = pl.ds(pl.multiple_of(me_row * chunk, chunk), chunk)
     total = part[my_rows, :]
     for d, copy in enumerate(rs_copies):
@@ -177,44 +272,41 @@
     ]
     for copy in w_copies:
         copy.start()
+    lab_gather.forward_rest()
     for copy in w_copies:
         copy.wait()
-    own_lab.wait()
-    for copy in lab_copies:
-        copy.wait()
+    lab_gather.finish()
 
     def blend(acc, block):
         return (mixing * acc + (1.0 - mixing) * lab_ref[block].astype(jnp.float32)).astype(
             jnp.bfloat16
         )
 
-    def first_round(b, _):
+    def first_round(h, b, _):
         rows = pl.ds(pl.multiple_of(b * BLOCK, BLOCK), BLOCK)
         weights = w_all[rows, :].astype(jnp.float32)
-        for h in range(2):
-            block = b + h * pairs
-            acc = jnp.zeros((BLOCK, classes), jnp.float32)
-            for k in range(0, SLOTS, 2):
-                pieces = []
-                for u in range(k, k + 2):
-                    index = (code[h * 4 + u // 4, rows, :] >> (8 * (u % 4))) & 0x7F
-                    pieces.append(lane_pick(weights, index).astype(jnp.bfloat16))
-                wide = jnp.concatenate(pieces, axis=1)
-                dense[block, :, k * BLOCK : (k + 2) * BLOCK] = wide
-                cand = jnp.concatenate(
-                    [lab_all[pattern_ref[block, k]], lab_all[pattern_ref[block, k + 1]]], axis=0
-                )
-                acc += jnp.dot(wide, cand, preferred_element_type=jnp.float32)
-            spread_all[me_col * blocks + block] = blend(acc, block)
+        block = b + h * pairs
+        acc = jnp.zeros((BLOCK, classes), jnp.float32)
+        for k in range(0, SLOTS, 2):
+            pieces = []
+            for u in range(k, k + 2):
+                index = (code[h * 4 + u // 4, rows, :] >> (8 * (u % 4))) & 0x7F
+                pieces.append(lane_pick(weights, index).astype(jnp.bfloat16))
+            wide = jnp.concatenate(pieces, axis=1)
+            dense[block, :, k * BLOCK : (k + 2) * BLOCK] = wide
+            cand = jnp.concatenate(
+                [lab_all[pattern_ref[block, k]], lab_all[pattern_ref[block, k + 1]]], axis=0
+            )
+            acc += jnp.dot(wide, cand, preferred_element_type=jnp.float32)
+        spread_all[me_col * blocks + block] = blend(acc, block)
         return 0
 
-    lax.fori_loop(0, pairs, first_round, 0)
-
-    spread_copies = gather_copies(spread_all.at[mine], spread_all, spread_send, spread_recv)
-    for copy in spread_copies:
-        copy.start()
-    for copy in spread_copies:
-        copy.wait()
+    for h in range(2):
+        lax.fori_loop(0, pairs, functools.partial(first_round, h), 0)
+        spread_gather.start_half(h)
+    spread_gather.forward_first()
+    spread_gather.forward_rest()
+    spread_gather.finish()
 
     def second_round(block, _):
         acc = jnp.zeros((BLOCK, classes), jnp.float32)
@@ -249,6 +341,7 @@
     lab = lax.dynamic_slice_in_dim(labels, row_pos * per_device, per_device, 1)
     lab = jnp.pad(lab, ((0, 0), (0, wide - per_device))).reshape(blocks, BLOCK, wide)
     pos = jnp.pad(mask_pos, ((0, 0), (1, HALF - 1 - neighbours)), constant_values=-1)
+    post = pos.T
     pos = jnp.concatenate([pos[:packed], pos[packed:]], axis=1)
     sharp = jnp.concatenate(
         [
@@ -262,25 +355,27 @@
     out = pl.pallas_call(
         functools.partial(kernel, n_row, n_col, neighbours, width),
         out_shape=jax.ShapeDtypeStruct((blocks, BLOCK, wide), jnp.bfloat16),
-        in_specs=[pl.BlockSpec(memory_space=pltpu.SMEM)] + [vmem] * 5,
+        in_specs=[pl.BlockSpec(memory_space=pltpu.SMEM)] + [vmem] * 6,
         out_specs=vmem,
         scratch_shapes=[
             pltpu.VMEM((total_blocks, features, BLOCK), jnp.bfloat16),
             pltpu.VMEM((total_blocks, BLOCK, wide), jnp.bfloat16),
             pltpu.VMEM((total_blocks, BLOCK, wide), jnp.bfloat16),
             pltpu.VMEM((8, packed, LANES), jnp.int32),
+            pltpu.VMEM((4, BLOCK, BLOCK), jnp.int32),
+            pltpu.VMEM((5, HALF, BLOCK), jnp.int32),
             pltpu.VMEM((packed, LANES), jnp.float32),
             pltpu.VMEM((n_row, packed // n_row, LANES), jnp.float32),
             pltpu.VMEM((packed, LANES), jnp.bfloat16),
             pltpu.VMEM((blocks, BLOCK, SLOTS * BLOCK), jnp.bfloat16),
             pltpu.SemaphoreType.DMA((2,)),
         ]
-        + [pltpu.SemaphoreType.DMA((n_col,))] * 6
+        + [pltpu.SemaphoreType.DMA((max(n_col, 14),))] * 6
         + [pltpu.SemaphoreType.DMA((n_row,))] * 4,
         compiler_params=pltpu.CompilerParams(
             collective_id=0, has_side_effects=True, vmem_limit_bytes=48 * 1024 * 1024
         ),
-    )(pattern, query, emb, lab, pos, sharp)
+    )(pattern, query, emb, lab, pos, post, sharp)
     return out.reshape(rows_here, wide)[:, :per_device]
 
 

time: 112 us -> 63.5 us (0.57)
  Pallas kernels: 108 us -> 55.6 us
  local copies, waits for them, and re-layouts: 3.58 us -> 7.35 us
    pallas_call x1, Pallas kernels: 108 us -> 55.6 us  [body(): pl.pallas_call(functools.partial(kernel, n_row, n_col, neighbours, width)...]
where the time goes in v2:
time: 63.5 us; the launch traced here: 63.2 us
  Pallas kernels  55.6 us (88%)
  local copies, waits for them, and re-layouts  7.35 us (12%)
    pallas_call x1, Pallas kernels, body(): pl.pallas_call(functools.partial(kernel, n_row, n_col, neighbours, width)...  55.6 us
    unnamed x6, local copies, waits for them, and re-layouts  1.92 us

profile of v2, /device:TPU:1, one launch (start us, length us, event | category | flops | bytes accessed | tf_op | source)
XLA Modules:
  0.0 63.2 jit_solution(15670020759416274845)
XLA Ops:
  0.0 0.0 copy-start
  0.0 0.8 %fusion = (f32[384]{0:T(512)S(1)}, f32[384]{0:T(512)S(1)}) fusion(f32[768]{0:T(1024)} %param.7), kind=kLoop, calls=%fused_computation.7 | loop fusion | bytes 6144 | tf_op jit(solution)/shard_map/slice | solution.py:348
  0.8 0.1 broadcast_in_dim.4
  0.9 0.1 broadcast_in_dim.5
  1.1 0.1 pad_maximum_fusion.sharp_ref
  1.2 0.9 %pad_bitcast_fusion.post_ref = s32[64,768]{1,0:T(8,128)S(1)} fusion(s32[768,50]{0,1:T(8,128)} %param.9), kind=kLoop, calls=%fused_computation | loop fusion | bytes 350208 | tf_op jit(solution)/shard_map/transpose | solution.py:344
  2.1 0.9 %pad_slice_fusion.1 = (s32[384,64]{0,1:T(8,128)S(1)}, s32[384,64]{0,1:T(8,128)S(1)}) fusion(s32[768,50]{0,1:T(8,128)} %param.9), kind=kLoop, calls=%fused_computation.2 | loop fusion | bytes 350208 | tf_op jit(solution)/shard_map/slice | solution.py:345
  3.1 0.1 copy.11.pos_ref
  3.2 1.2 %constant_dynamic-slice_fusion.1.query_ref = bf16[768,192]{1,0:T(8,128)(2,1)S(1)} fusion(bf16[768,768]{1,0:T(8,128)(2,1)} %param.5, s32[]{:T(128)S(6)} %select_n.6), kind=kLoop, calls=%fused_computation.6 | loop fusion | bytes 589828 | tf_op jit(solution)/shard_map/dynamic_slice | solution.py:339
  4.5 0.0 copy-start.1
  4.5 0.2 copy.9
  4.7 0.0 copy-done
  4.7 0.8 %constant_dynamic-slice_fusion = bf16[768,250]{0,1:T(8,128)(2,1)} fusion(bf16[768,1000]{0,1:T(8,128)(2,1)S(1)} %copy-done, s32[]{:T(128)S(6)} %select_n.7), kind=kLoop, calls=%fused_computation.5 | loop fusion | bytes 768004 | tf_op jit(solution)/shard_map/dynamic_slice | solution.py:341
  5.6 1.2 %copy.14 = bf16[768,250]{1,0:T(8,128)(2,1)S(1)} copy(bf16[768,250]{0,1:T(8,128)(2,1)} %constant_dynamic-slice_fusion) | data formatting | bytes 768000
  6.8 0.1 pad.8.clone
  6.8 0.0 copy-done.1
  6.8 55.6 %shard_map.55 = bf16[6,128,256]{2,1,0:T(8,128)(2,1)S(1)} custom-call(s32[6,16]{1,0:T(8,128)S(1)} %copy-done.1, bf16[768,192]{1,0:T(8,128)(2,1)S(1)} %constant_dynamic-slice_fusion.1.query_ref, bf16[6,192,128]{2,1,0:T(8,128)(2,1)S(1)} %bitcast.10, bf16[6,128,256]{2,1,0:T(8,128)(2,1)S(1)} %bitcast.9, s32[384,128]{1,0:T(8,128)S(1)} %copy.11.pos_ref, ...), custom_call_target="tpu_custom_call" | custom-call | tf_op jit(solution)/shard_map/pallas_call | solution.py:355
  62.4 0.7 %copy.16 = bf16[768,250]{1,0:T(8,128)(2,1)} copy(bf16[768,250]{1,0:T(8,128)(2,1)S(1)} %bitcast.8) | data formatting | bytes 768000
  (1 shorter events, 0.0 us)
Async XLA Ops:
  0.0 4.7 %copy-start = (bf16[768,1000]{0,1:T(8,128)(2,1)S(1)}, bf16[768,1000]{0,1:T(8,128)(2,1)}, u32[]{:S(2)}) copy-start(bf16[768,1000]{0,1:T(8,128)(2,1)} %param.6) | copy-start | bytes 4608004
  4.5 2.3 %copy-start.1 = (s32[6,16]{1,0:T(8,128)S(1)}, s32[6,16]{1,0:T(8,128)}, u32[]{:S(2)}) copy-start(s32[6,16]{1,0:T(8,128)} %pattern_ref.1) | copy-start | bytes 1156

commit v3 on v2

--- a/solution.py
+++ b/solution.py
@@ -132,8 +132,8 @@
 
 def kernel(
     n_row, n_col, neighbours, width,
-    pattern_ref, query_ref, emb_ref, lab_ref, pos_ref, post_ref, sharp_ref, out_ref,
-    emb_all, lab_all, spread_all, code, turned, number, part, rs_buf, w_all, dense,
+    pattern_ref, query_ref, emb_ref, lab_ref, post_ref, sharpt_ref, out_ref,
+    pos_ref, sharp_ref, emb_all, lab_all, spread_all, code, turned, number, part, rs_buf, w_all, dense,
     local_sem, emb_send, emb_recv, lab_send, lab_recv, spread_send, spread_recv,
     rs_send, rs_recv, w_send, w_recv,
 ):
@@ -165,6 +165,18 @@
 
     tile = 32
     emb_gather.start()
+
+    for b in range(pairs):
+        rows = slice(b * BLOCK, (b + 1) * BLOCK)
+        others = slice((b + pairs) * BLOCK, (b + pairs + 1) * BLOCK)
+        pos_ref[rows, :] = jnp.concatenate([post_ref[:, rows], post_ref[:, others]], axis=0).T
+        sharp_ref[rows, :] = jnp.concatenate(
+            [
+                jnp.broadcast_to(sharpt_ref[:, rows], (HALF, BLOCK)),
+                jnp.broadcast_to(sharpt_ref[:, others], (HALF, BLOCK)),
+            ],
+            axis=0,
+        ).T
 
     def encode(block, _):
         cols = pl.ds(pl.multiple_of(block * BLOCK, BLOCK), BLOCK)
@@ -342,22 +354,17 @@
     lab = jnp.pad(lab, ((0, 0), (0, wide - per_device))).reshape(blocks, BLOCK, wide)
     pos = jnp.pad(mask_pos, ((0, 0), (1, HALF - 1 - neighbours)), constant_values=-1)
     post = pos.T
-    pos = jnp.concatenate([pos[:packed], pos[packed:]], axis=1)
-    sharp = jnp.concatenate(
-        [
-            jnp.broadcast_to(sharpness[:packed, None], (packed, HALF)),
-            jnp.broadcast_to(sharpness[packed:, None], (packed, HALF)),
-        ],
-        axis=1,
-    )
+    sharpt = sharpness.reshape(1, rows_here)
     total_blocks = n_col * blocks
     vmem = pl.BlockSpec(memory_space=pltpu.VMEM)
     out = pl.pallas_call(
         functools.partial(kernel, n_row, n_col, neighbours, width),
         out_shape=jax.ShapeDtypeStruct((blocks, BLOCK, wide), jnp.bfloat16),
-        in_specs=[pl.BlockSpec(memory_space=pltpu.SMEM)] + [vmem] * 6,
+        in_specs=[pl.BlockSpec(memory_space=pltpu.SMEM)] + [vmem] * 5,
         out_specs=vmem,
         scratch_shapes=[
+            pltpu.VMEM((packed, LANES), jnp.int32),
+            pltpu.VMEM((packed, LANES), jnp.float32),
             pltpu.VMEM((total_blocks, features, BLOCK), jnp.bfloat16),
             pltpu.VMEM((total_blocks, BLOCK, wide), jnp.bfloat16),
             pltpu.VMEM((total_blocks, BLOCK, wide), jnp.bfloat16),
@@ -375,7 +382,7 @@
         compiler_params=pltpu.CompilerParams(
             collective_id=0, has_side_effects=True, vmem_limit_bytes=48 * 1024 * 1024
         ),
-    )(pattern, query, emb, lab, pos, post, sharp)
+    )(pattern, query, emb, lab, post, sharpt)
     return out.reshape(rows_here, wide)[:, :per_device]
 
 

time: 63.5 us -> 60.3 us (0.950)
  local copies, waits for them, and re-layouts: 7.35 us -> 4.39 us
    slice x2 -> x0, local copies, waits for them, and re-layouts: 1.77 us -> none  [the longest x1 0.95 us: body(): pos = jnp.concatenate([pos[:packed], pos[packed:]], axis=1)]
    unnamed x6, local copies, waits for them, and re-layouts: 1.92 us -> 1.03 us
    reshape x0 -> x1, local copies, waits for them, and re-layouts: none -> 0.81 us  [body(): sharpt = sharpness.reshape(1, rows_here)]
    dynamic_slice x1, local copies, waits for them, and re-layouts: 0.85 us -> 0.1 us  [body(): lab = lax.dynamic_slice_in_dim(labels, row_pos * per_device, per_device, 1)]
where the time goes in v3:
time: 60.3 us; the launch traced here: 60 us
  Pallas kernels  55.6 us (92%)
  local copies, waits for them, and re-layouts  4.39 us (7%)
    pallas_call x1, Pallas kernels, body(): pl.pallas_call(functools.partial(kernel, n_row, n_col, neighbours, width)...  55.6 us
    dynamic_slice x1, local copies, waits for them, and re-layouts, body(): query = lax.dynamic_slice_in_dim(embeds, row_pos * features, features, 1)  1.25 us

profile of v3, /device:TPU:1, one launch (start us, length us, event | category | flops | bytes accessed | tf_op | source)
XLA Modules:
  0.0 60.0 jit_solution(4518694674626345735)
XLA Ops:
  0.0 0.0 copy-start
  0.0 0.8 %reshape.14.sharpt_ref = f32[1,768]{1,0:T(1,128)S(1)} reshape(f32[768]{0:T(1024)} %param.7) | data formatting | bytes 6144 | tf_op jit(solution)/shard_map/reshape | solution.py:357
  0.8 0.9 %pad_bitcast_fusion.post_ref = s32[64,768]{1,0:T(8,128)S(1)} fusion(s32[768,50]{0,1:T(8,128)} %param.9), kind=kLoop, calls=%fused_computation | loop fusion | bytes 350208 | tf_op jit(solution)/shard_map/transpose | solution.py:356
  1.7 1.2 %constant_dynamic-slice_fusion.1.query_ref = bf16[768,192]{1,0:T(8,128)(2,1)S(1)} fusion(bf16[768,768]{1,0:T(8,128)(2,1)} %param.5, s32[]{:T(128)S(6)} %select_n.6), kind=kLoop, calls=%fused_computation.2 | loop fusion | bytes 589828 | tf_op jit(solution)/shard_map/dynamic_slice | solution.py:351
  3.0 0.0 copy-start.1
  3.0 0.2 copy.8
  3.2 0.0 copy-done
  3.2 0.1 constant_dynamic-slice_fusion
  3.3 0.2 copy.12
  3.5 0.1 pad.8.clone
  3.6 0.1 copy-done.1
  3.7 55.6 %shard_map.55 = bf16[6,128,256]{2,1,0:T(8,128)(2,1)S(1)} custom-call(s32[6,16]{1,0:T(8,128)S(1)} %copy-done.1, bf16[768,192]{1,0:T(8,128)(2,1)S(1)} %constant_dynamic-slice_fusion.1.query_ref, bf16[6,192,128]{2,1,0:T(8,128)(2,1)S(1)} %bitcast.10, bf16[6,128,256]{2,1,0:T(8,128)(2,1)S(1)} %bitcast.9, s32[64,768]{1,0:T(8,128)S(1)} %pad_bitcast_fusion.post_ref, ...), custom_call_target="tpu_custom_call" | custom-call | tf_op jit(solution)/shard_map/pallas_call | solution.py:360
  59.3 0.7 %copy.14 = bf16[768,250]{1,0:T(8,128)(2,1)} copy(bf16[768,250]{1,0:T(8,128)(2,1)S(1)} %bitcast.8) | data formatting | bytes 768000
Async XLA Ops:
  0.0 3.2 %copy-start = (bf16[768,1000]{0,1:T(8,128)(2,1)S(1)}, bf16[768,1000]{0,1:T(8,128)(2,1)}, u32[]{:S(2)}) copy-start(bf16[768,1000]{0,1:T(8,128)(2,1)} %param.6) | copy-start | bytes 4608004
  3.0 0.7 %copy-start.1 = (s32[6,16]{1,0:T(8,128)S(1)}, s32[6,16]{1,0:T(8,128)}, u32[]{:S(2)}) copy-start(s32[6,16]{1,0:T(8,128)} %pattern_ref.1) | copy-start | bytes 1156

commit v4 on v3

--- a/solution.py
+++ b/solution.py
@@ -202,9 +202,11 @@
             code[side * 4 + q, rows, :] = turned[q].T
         return 0
 
-    lax.fori_loop(0, pairs, encode, 0)
+    early = blocks // 3
+    late = blocks - 2
+    lax.fori_loop(0, early, encode, 0)
     emb_gather.forward_first()
-    lax.fori_loop(pairs, blocks, encode, 0)
+    lax.fori_loop(early, late, encode, 0)
     emb_gather.forward_rest()
     lab_gather.start()
     emb_gather.finish()
@@ -251,6 +253,7 @@
     for copy in rs_copies:
         copy.start()
     lab_gather.forward_first()
+    lax.fori_loop(late, late + 1, encode, 0)
     my_rows = pl.ds(pl.multiple_of(me_row * chunk, chunk), chunk)
     total = part[my_rows, :]
     for d, copy in enumerate(rs_copies):
@@ -284,6 +287,7 @@
     ]
     for copy in w_copies:
         copy.start()
+    lax.fori_loop(late + 1, blocks, encode, 0)
     lab_gather.forward_rest()
     for copy in w_copies:
         copy.wait()

time: 60.3 us -> 60.3 us (level)
  no operation moved by 1% of the time
where the time goes in v4:
time: 60.3 us; the launch traced here: 60 us
  Pallas kernels  55.5 us (92%)
  local copies, waits for them, and re-layouts  4.39 us (7%)
    pallas_call x1, Pallas kernels, body(): pl.pallas_call(functools.partial(kernel, n_row, n_col, neighbours, width)...  55.5 us
    dynamic_slice x1, local copies, waits for them, and re-layouts, body(): query = lax.dynamic_slice_in_dim(embeds, row_pos * features, features, 1)  1.25 us

profile of v4, /device:TPU:1, one launch (start us, length us, event | category | flops | bytes accessed | tf_op | source)
XLA Modules:
  0.0 60.0 jit_solution(8330038174361613109)
XLA Ops:
  0.0 0.0 copy-start
  0.0 0.8 %reshape.14.sharpt_ref = f32[1,768]{1,0:T(1,128)S(1)} reshape(f32[768]{0:T(1024)} %param.7) | data formatting | bytes 6144 | tf_op jit(solution)/shard_map/reshape | solution.py:361
  0.8 0.9 %pad_bitcast_fusion.post_ref = s32[64,768]{1,0:T(8,128)S(1)} fusion(s32[768,50]{0,1:T(8,128)} %param.9), kind=kLoop, calls=%fused_computation | loop fusion | bytes 350208 | tf_op jit(solution)/shard_map/transpose | solution.py:360
  1.7 1.2 %constant_dynamic-slice_fusion.1.query_ref = bf16[768,192]{1,0:T(8,128)(2,1)S(1)} fusion(bf16[768,768]{1,0:T(8,128)(2,1)} %param.5, s32[]{:T(128)S(6)} %select_n.6), kind=kLoop, calls=%fused_computation.2 | loop fusion | bytes 589828 | tf_op jit(solution)/shard_map/dynamic_slice | solution.py:355
  3.0 0.0 copy-start.1
  3.0 0.2 copy.8
  3.2 0.0 copy-done
  3.2 0.1 constant_dynamic-slice_fusion
  3.3 0.2 copy.12
  3.5 0.1 pad.8.clone
  3.6 0.1 copy-done.1
  3.7 55.5 %shard_map.55 = bf16[6,128,256]{2,1,0:T(8,128)(2,1)S(1)} custom-call(s32[6,16]{1,0:T(8,128)S(1)} %copy-done.1, bf16[768,192]{1,0:T(8,128)(2,1)S(1)} %constant_dynamic-slice_fusion.1.query_ref, bf16[6,192,128]{2,1,0:T(8,128)(2,1)S(1)} %bitcast.10, bf16[6,128,256]{2,1,0:T(8,128)(2,1)S(1)} %bitcast.9, s32[64,768]{1,0:T(8,128)S(1)} %pad_bitcast_fusion.post_ref, ...), custom_call_target="tpu_custom_call" | custom-call | tf_op jit(solution)/shard_map/pallas_call | solution.py:364
  59.2 0.7 %copy.14 = bf16[768,250]{1,0:T(8,128)(2,1)} copy(bf16[768,250]{1,0:T(8,128)(2,1)S(1)} %bitcast.8) | data formatting | bytes 768000
Async XLA Ops:
  0.0 3.2 %copy-start = (bf16[768,1000]{0,1:T(8,128)(2,1)S(1)}, bf16[768,1000]{0,1:T(8,128)(2,1)}, u32[]{:S(2)}) copy-start(bf16[768,1000]{0,1:T(8,128)(2,1)} %param.6) | copy-start | bytes 4608004
  3.0 0.7 %copy-start.1 = (s32[6,16]{1,0:T(8,128)S(1)}, s32[6,16]{1,0:T(8,128)}, u32[]{:S(2)}) copy-start(s32[6,16]{1,0:T(8,128)} %pattern_ref.1) | copy-start | bytes 1156
